TPU v7x, 512 devices: a whole 4x4x16 slice. The times are simulated.
512 devices in a mesh: seq: 128 (over z, y, core), ch: 4 (over x).
Axes of the slice: x: 4, y: 4, z: 16, core: 2. Of those that a mesh axis runs over, the one named last changes fastest.
Arguments:
- q_stream: bfloat16 [16384, 4096], P('seq', 'ch'), may hold values from -6 to 6
- k_stream: bfloat16 [16384, 4096], P('seq', 'ch'), may hold values from -6 to 6
- v_stream: bfloat16 [16384, 4096], P('seq', 'ch'), may hold values from -6 to 6
- short_filter: float32 [3, 3, 4096], P(None, None, 'ch'), may hold values from -4 to 4
- rates: float32 [16, 4096], P(None, 'ch'), may hold values from 6.1035155e-07 to 0.03
- residues: float32 [16, 4096], P(None, 'ch'), may hold values from -3 to 3
- skip: float32 [4096], P('ch'), may hold values from -3 to 3
- prior_state: float32 [16, 4096], P(None, 'ch'), may hold values from -5 to 5
- out_weight: bfloat16 [4096, 4096], P('ch', 'seq'), may hold values from -0.375 to 0.375
- residual: bfloat16 [16384, 4096], P('seq', 'ch'), may hold values from -24 to 24
- norm_gain: float32 [4096], P('ch'), may hold values from 0.5 to 1.5
Outputs:
- hidden_out: bfloat16 [16384, 4096], P('seq', 'ch')
- normed: bfloat16 [16384, 4096], P('seq', 'ch')
All inputs are finite; a program needn't handle non-finite values.
Results may differ from a plain program's by a relative error of at most 0.005.
Values may be sent and summed in bfloat16 or wider, within the bound.
A program may use at most 128 MiB of HBM per device.

v0:
```python
import functools

import jax
import jax.numpy as jnp
from jax import lax
from jax.experimental import pallas as pl
from jax.experimental.pallas import tpu as pltpu
from jax.sharding import PartitionSpec as P

MESH = pl.DeviceIdType.MESH
F32 = jnp.float32
BF16 = jnp.bfloat16
NX, NY, NZ, NH = 4, 4, 16, 2
NJ = NY * NH
ROWS = 128
CHANS = 1024
LANES = 128
SUBS = 8
MODES = 16
BAND = CHANS // NX


def one_minus_exp(x):
    series = jnp.full_like(x, 1.0 / 8.0)
    for n in (7.0, 6.0, 5.0, 4.0, 3.0, 2.0):
        series = (1.0 - x * series) * (1.0 / n)
    return jnp.where(x < 0.25, x * (1.0 - x * series), 1.0 - jnp.exp(-x))


def kernel(
    q_hbm, k_hbm, v_hbm, taps_hbm, rates_hbm, residues_hbm, skip_hbm, prior_hbm, weight_hbm, residual_hbm, gain_hbm,
    hidden_ref, normed_ref,
    q_ref, k_ref, v_ref, taps_ref, rates_ref, residues_ref, skip_ref, prior_ref, residual_ref, gain_ref,
    streams, halo, gated, featq, filt, tap_rows, rate_rows, res_rows, prior_rows, pole_rows, inres_rows, inflow_rows,
    ends, plane_in, line_in, line_out, back_out, carry,
    weights, acts, far_out, far_in, near_out, near_in, parts, back_rows, final_in,
    res_out, res_in, summed, stat_out, stat_in,
    input_s, halo_s, halo_r, s1_s, s1_r, s2_s, s2_r, s3_s, s3_r, ring_s, ring_r, sib_s, sib_r,
    act_s, act_r, fwd_s, fwd_r, far_s, far_r, near_s, near_r,
    fin_s, fin_r, res_s, res_r, stat_s, stat_r,
):
    seq, x = lax.axis_index("seq"), lax.axis_index("ch")
    z, j = lax.div(seq, NJ), lax.rem(seq, NJ)
    y, h = lax.div(j, NH), lax.rem(j, NH)

    def device(z_, j_, x_):
        return (z_ * NJ + j_, x_)

    def remote(src, dst, send, recv, target):
        return pltpu.make_async_remote_copy(
            src_ref=src, dst_ref=dst, send_sem=send, recv_sem=recv, device_id=target, device_id_type=MESH
        )

    def row(t):
        return pl.ds(pl.multiple_of(t * SUBS, SUBS), SUBS)

    own_weights = weights.at[shard_rows(0, h), :]
    inputs = [
        pltpu.make_async_copy(src, dst, input_s.at[n])
        for n, (src, dst) in enumerate((
            (k_hbm, k_ref), (v_hbm, v_ref), (q_hbm, q_ref), (weight_hbm, own_weights), (rates_hbm, rates_ref),
            (taps_hbm, taps_ref), (residues_hbm, residues_ref), (prior_hbm, prior_ref), (skip_hbm, skip_ref),
            (residual_hbm, residual_ref), (gain_hbm, gain_ref),
        ))
    ]
    for copy in inputs[:4]:
        copy.start()

    barrier = pltpu.get_barrier_semaphore()

    def greet(target):
        pl.semaphore_signal(barrier, inc=1, device_id=target, device_id_type=MESH)

    sibling = device(z, y * NH + 1 - h, x)

    def along(hops, core):
        return device(lax.rem(z + hops + NZ, NZ), y * NH + core, x)

    for d in range(1, NZ):
        greet(along(d, h))
    for d in (1, -1, 2 - 4 * h):
        greet(along(d, 1 - h))
    for d in range(1, NJ):
        greet(device(z, lax.rem(j + d, NJ), x))
    for d in range(1, NX):
        for e in range(NY):
            greet(device(z, lax.rem(y + e, NY) * NH + h, lax.rem(x + d, NX)))

    has_next, has_prev = seq < NZ * NJ - 1, seq > 0
    first_j, last_j = j == 0, j == NJ - 1

    @pl.when(last_j)
    def _():
        greet(device(lax.rem(z + 1, NZ), 0, x))

    @pl.when(first_j)
    def _():
        greet(device(lax.rem(z + NZ - 1, NZ), NJ - 1, x))

    for copy in inputs[4:]:
        copy.start()

    def shard(slot):
        return weights.at[shard_rows(slot, h), :]

    def ring_copy(src, hops, slot, sent, got, core=None):
        to = along(hops, h if core is None else core)
        return remote(src, shard(slot), ring_s.at[sent], ring_r.at[got], to)

    def ring_first():
        for d in (2, 1):
            ring_copy(weight_hbm, d, NZ - d, 0, 0 if d == 2 else 2).start()
            ring_copy(weight_hbm, -d, d, 0, 1 if d == 2 else 2).start()
        remote(weight_hbm, own_weights, sib_s.at[0], sib_r.at[0], sibling).start()

    def shards_all(count, sent, got):
        some = weights.at[pl.ds(0, count * 32), :]
        return remote(some, some, ring_s.at[sent], ring_r.at[got], sibling)

    def shards_wait(count, got):
        shards_all(count, 0, got).wait_recv()

    def ring_next(step):
        far, got = 2 * step, 3 * step
        shards_wait(1, got - 3)
        for d in (2, 1):
            ring_copy(shard(NZ - far), d, NZ - far - d, step, got if d == 2 else got + 2).start()
        shards_wait(1, got - 2)
        for d in (2, 1):
            ring_copy(shard(far), -d, far + d, step, got + 1 if d == 2 else got + 2).start()

    def ring_last():
        shards_wait(1, 6)
        shards_wait(1, 7)
        for core in (h, 1 - h):
            ring_copy(shard(NZ - 6 - 4 * h), 2 - 4 * h, 8, 3, 9, core).start()
        for core in (h, 1 - h):
            ring_copy(shard(NZ - 6), 1, NZ - 7, 3, 9, core).start()
            ring_copy(shard(6), -1, 7, 3, 9, core).start()

    def sib_copy(slot):
        two = weights.at[pl.ds(pl.multiple_of(h * (NZ * 32) + slot * 32, 32), 2 * 32), :]
        return remote(two, two, sib_s.at[1], sib_r.at[1], sibling)

    def sib_give(step):
        shards_wait(2, 3 * step - 1)
        sib_copy(NZ - 2 * step).start()
        sib_copy(2 * step - 1).start()

    peers = NJ - 1 + (NX - 1) * NY + NZ - 1 + 3
    edge = jnp.logical_or(first_j, last_j)
    early = z < 7

    def convert(stream, ref, begin, end):
        for part in range(SUBS):
            to = pl.ds(begin * SUBS + part, end - begin, stride=SUBS)
            streams[stream, to, :] = ref[begin:end, part * LANES : (part + 1) * LANES].astype(F32)

    for n in range(3):
        inputs[n].wait()
    for stream, ref in enumerate((q_ref, k_ref, v_ref)):
        convert(stream, ref, ROWS - 16, ROWS)
    last = (ROWS - 2) * SUBS
    halo_copy = remote(
        streams.at[:, pl.ds(last, 2 * SUBS), :], halo, halo_s, halo_r, (lax.rem(seq + 1, NZ * NJ), x)
    )
    convert(1, k_ref, 0, ROWS - 16)
    convert(2, v_ref, 0, ROWS - 16)
    for n in range(3, len(inputs)):
        inputs[n].wait()

    for part in range(SUBS):
        cut = slice(part * LANES, (part + 1) * LANES)
        to = pl.ds(part, MODES, stride=SUBS)
        rate_rows[to, :] = rates_ref[:, cut]
        res_rows[to, :] = residues_ref[:, cut]
        prior_rows[to, :] = prior_ref[:, cut]
        for stream in range(3):
            for tap in range(3):
                n = (3 * stream + tap) * SUBS + part
                tap_rows[n : n + 1, :] = taps_ref[stream, tap : tap + 1, cut]
    rates = rate_rows[...]
    inflow = jnp.sqrt(one_minus_exp(2.0 * rates))
    pole_rows[...] = jnp.exp(-rates)
    inflow_rows[...] = inflow
    inres_rows[...] = res_rows[...] * inflow

    def modes_of(ref):
        return [ref[m * SUBS : (m + 1) * SUBS, :] for m in range(MODES)]

    taps = [tap_rows[n * SUBS : (n + 1) * SUBS, :] for n in range(9)]
    poles = modes_of(pole_rows)
    skip = skip_ref[...]

    def feature(stream, now, back1, back2):
        return taps[3 * stream] * now + taps[3 * stream + 1] * back1 + taps[3 * stream + 2] * back2

    def gate(t, history):
        later, feats = [], []
        for stream, (back1, back2) in zip((1, 2), history):
            now = streams[stream, row(t), :]
            feats.append(feature(stream, now, back1, back2))
            later.append((now, back1))
        value = feats[0] * feats[1]
        gated[row(t), :] = value
        return value, tuple(later)

    def steps(begin, end, step, carried):
        def eight(block, carried):
            for t in range(8):
                carried = step(block * 8 + t, carried)
            return carried

        return lax.fori_loop(begin // 8, end // 8, eight, carried)

    def advance(states, value):
        return tuple(pole * state + value for pole, state in zip(poles, states))

    history = tuple((streams[s, SUBS : 2 * SUBS, :], streams[s, 0:SUBS, :]) for s in (1, 2))
    states = tuple(jnp.zeros((SUBS, LANES), F32) for _ in range(MODES))

    def scan_step(t, carried):
        states, history = carried
        value, history = gate(t, history)
        return advance(states, value), history

    scan = (states, history)
    for t in range(2, 8):
        scan = scan_step(t, scan)
    states, history = steps(8, ROWS, scan_step, scan)

    @pl.when(edge)
    def _():
        pl.semaphore_wait(barrier, peers + 1)

    @pl.when(jnp.logical_not(edge))
    def _():
        pl.semaphore_wait(barrier, peers)

    pl.when(has_next)(halo_copy.start)
    ring_first()

    for tile in range(SUBS):
        turned = residual_ref[:, tile * LANES : (tile + 1) * LANES].astype(F32).T.astype(BF16)
        to_rows = slice((tile // 2) * 64, (tile // 2) * 64 + 64)
        for odd in range(2):
            res_out[2 * (tile % 2) + odd, to_rows, :] = turned[64 * odd : 64 * odd + 64, :]

    def beside(block, dx=0):
        return device(z, lax.rem(y + (0, 3, 1, 2)[block], NY) * NH + h, x if dx == 0 else lax.rem(x + dx, NX))

    def res_copy(block):
        to = lax.rem(y + (0, 1, 3, 2)[block], NY)
        return remote(res_out.at[to], res_in.at[block - 1], res_s, res_r, device(z, to * NH + h, x))

    for block in range(1, 4):
        res_copy(block).start()
    convert(0, q_ref, 0, ROWS - 16)

    @pl.when(has_prev)
    def _():
        halo_copy.wait_recv()

    @pl.when(jnp.logical_not(has_prev))
    def _():
        halo[...] = jnp.zeros_like(halo)

    def halo_rows(s):
        return halo[s, SUBS : 2 * SUBS, :], halo[s, 0:SUBS, :]

    first, history = gate(0, (halo_rows(1), halo_rows(2)))
    second, history = gate(1, history)
    for m in range(MODES):
        at = slice(m * SUBS, (m + 1) * SUBS)
        late = jnp.exp(-(ROWS - 2.0) * rate_rows[at, :])
        ends[at, :] = inflow_rows[at, :] * (states[m] + late * (poles[m] * first + second))

    pair = 2 * SUBS

    def pair_rows(n):
        return pl.ds(pl.multiple_of(n * pair, pair), pair)

    def to_owner(d):
        to = lax.rem(j + d, NJ)
        return remote(ends.at[pair_rows(to), :], plane_in.at[j], s1_s, s1_r, device(z, to, x))

    def along_line(d):
        return remote(line_out, line_in.at[z], s2_s.at[d], s2_r.at[d], along(d, h))

    def from_owner(d):
        to = lax.rem(j + d, NJ)
        return remote(back_out.at[to], carry.at[pair_rows(j), :], s3_s, s3_r, device(z, to, x))

    for d in range(1, NJ):
        to_owner(d).start()

    plane_in[j] = ends[pair_rows(j), :]

    inres = modes_of(inres_rows)

    def output_step(t, carried):
        states, (back1, back2) = carried
        now = streams[0, row(t), :]
        featq[row(t), :] = feature(0, now, back1, back2)
        value = gated[row(t), :]
        states = advance(states, value)
        terms = [r * s for r, s in zip(inres, states)] + [skip * value]
        filt[row(t), :] = tree_sum(terms)
        return states, (now, back1)

    states = tuple(jnp.zeros((SUBS, LANES), F32) for _ in range(MODES))
    outputs = steps(0, 64, output_step, (states, halo_rows(0)))
    ring_next(1)

    others = plane_in.at[pl.ds(0, NJ - 1)]
    to_owner_all = remote(others, others, s1_s, s1_r, sibling)
    to_owner_all.wait_recv()

    my_rates = rate_rows[pair_rows(j), :]
    block_decay = jnp.exp(-float(ROWS) * my_rates)
    plane_decay = jnp.exp(-float(ROWS * NJ) * my_rates)
    total = plane_in[0]
    for i in range(1, NJ):
        total = block_decay * total + plane_in[i]
    line_out[...] = total

    @pl.loop(1, NZ - z)
    def _(d):
        along_line(d).start()

    late = jnp.logical_not(early)

    @pl.when(late)
    def _():
        ring_next(2)
        sib_give(1)

    steps(64, ROWS, output_step, outputs)
    pl.when(late)(ring_last)

    @pl.loop(1, z + 1)
    def _(d):
        along_line(d).wait_recv()

    incoming = lax.fori_loop(0, z, lambda i, s: plane_decay * s + line_in[i], prior_rows[pair_rows(j), :])
    for i in range(NJ):
        back_out[i] = incoming
        incoming = block_decay * incoming + plane_in[i]

    for d in range(1, NJ):
        from_owner(d).start()

    carry[pair_rows(j), :] = back_out[j]


    others = back_out.at[pl.ds(0, NJ - 1)]
    from_owner_all = remote(others, others, s3_s, s3_r, sibling)
    from_owner_all.wait_recv()

    half = ROWS // 2
    up = device(z, lax.rem(y + 1, NY) * NH + h, x)
    down = device(z, lax.rem(y + 3, NY) * NH + h, x)
    across = device(z, lax.rem(y + 2, NY) * NH + h, x)

    act_wait = (0, 2, 2, 1)

    def act_copy(part, side):
        cut = pl.ds(part * half, half)
        n = 2 * part + side
        return remote(acts.at[0, cut, :], acts.at[1 + side, cut, :], act_s, act_r.at[act_wait[n]], (up, down)[side])

    def fwd_copy(part):
        cut = pl.ds(part * half, half)
        return remote(acts.at[1 + part, cut, :], acts.at[3, cut, :], fwd_s, fwd_r, (up, down)[part])

    def carried_step(t, waves):
        waves = tuple(pole * wave for pole, wave in zip(poles, waves))
        filt[row(t), :] = featq[row(t), :] * (filt[row(t), :] + tree_sum(list(waves)))
        return waves

    waves = tuple(res_rows[m * SUBS : (m + 1) * SUBS, :] * carry[m * SUBS : (m + 1) * SUBS, :] for m in range(MODES))
    for part in range(2):
        waves = steps(part * half, (part + 1) * half, carried_step, waves)
        for sub in range(SUBS):
            from_rows = pl.ds(part * half * SUBS + sub, half, stride=SUBS)
            acts[0, part * half : (part + 1) * half, sub * LANES : (sub + 1) * LANES] = filt[from_rows, :].astype(BF16)
        act_copy(part, part).start()
    act_copy(1, 0).start()
    act_copy(0, 1).start()

    @pl.when(early)
    def _():
        ring_next(2)
        sib_give(1)
        ring_last()

    pl.when(has_next)(halo_copy.wait_send)
    to_owner_all.wait_send()
    from_owner_all.wait_send()

    @pl.loop(1, NZ - z)
    def _(d):
        along_line(d).wait_send()

    sib_give(2)
    sib_give(3)
    own_all = remote(weight_hbm, own_weights, sib_s.at[0], sib_r.at[0], sibling)
    own_all.wait_send()
    own_all.wait_recv()
    for sent in range(3):
        shards_all(4, sent, 0).wait_send()
    res_all = remote(res_in, res_in, res_s, res_r, sibling)
    res_all.wait_send()
    res_all.wait_recv()
    for part in range(2):
        act_copy(part, part).wait_recv()
        fwd_copy(part).start()
    shards_wait(6, 9)
    twelve = weights.at[pl.ds(0, 12 * 32), :]
    sib_all = remote(twelve, twelve, sib_s.at[1], sib_r.at[1], sibling)
    sib_all.wait_recv()

    right, left = device(z, j, lax.rem(x + 1, NX)), device(z, j, lax.rem(x + 3, NX))
    sides = (right, left)

    def project(pair):
        rows = acts[2 * pair : 2 * pair + 2].reshape(2 * ROWS, CHANS)
        parts[pair] = lax.dot_general(weights[...], rows, (((1,), (1,)), ((), ())), preferred_element_type=F32)

    def band(pair, dx):
        first = lax.rem(x + dx, NX) * 4 + NZ - z
        slots = [lax.rem(first + i, NZ) for i in range(4)]
        return [parts[pair, shard_rows(slot, core), :] for slot in slots for core in range(2)]

    def far_copy(pair, side):
        n = 2 * pair + side
        return remote(far_out.at[n], far_in.at[n], far_s.at[pair], far_r.at[pair], sides[side])

    def near_copy(pair, side):
        n = 2 * pair + side
        return remote(near_out.at[n], near_in.at[n], near_s.at[pair], near_r.at[pair], sides[side])

    def far_all(pair):
        both = far_in.at[pl.ds(2 * pair, 2)]
        return remote(both, both, far_s.at[pair], far_r.at[pair], right)

    def near_all(pair):
        both = near_in.at[pl.ds(2 * pair, 2)]
        return remote(both, both, near_s.at[pair], near_r.at[pair], right)

    def begin(pair):
        project(pair)
        chunks = band(pair, 2)
        for side in range(2):
            for i in range(4):
                far_out[2 * pair + side, 32 * i : 32 * i + 32, :] = chunks[4 * side + i].astype(BF16)
            far_copy(pair, side).start()

    def middle(pair):
        far_all(pair).wait_recv()
        for side in range(2):
            n = 2 * pair + side
            for i, chunk in enumerate(band(pair, (1, 3)[side])):
                if i // 4 == side:
                    chunk = chunk + far_in[n, 32 * (i % 4) : 32 * (i % 4) + 32, :].astype(F32)
                near_out[n, 32 * i : 32 * i + 32, :] = chunk.astype(BF16)
            near_copy(pair, side).start()

    def fin_copy(block):
        return remote(back_rows.at[block - 1], final_in.at[y], fin_s, fin_r, beside(block))

    def stat_copy(block, dx):
        n = 4 * block + dx
        return remote(stat_out.at[block], stat_in.at[n], stat_s, stat_r, beside(block, dx))

    def finish(pair):
        near_all(pair).wait_recv()
        value = jnp.concatenate(band(pair, 0), axis=0)
        for side in range(2):
            value = value + near_in[2 * pair + side].astype(F32)
        for block in (2 * pair + 1, 2 * pair):
            lanes = slice(block % 2 * ROWS, (block % 2 + 1) * ROWS)
            if block == 0:
                part = value[:, lanes] + res_out[y].astype(F32)
                final_in[y] = part.astype(BF16)
            else:
                part = value[:, lanes] + res_in[block - 1].astype(F32)
                back_rows[block - 1] = part.astype(BF16)
                fin_copy(block).start()
            squares = jnp.sum(part * part, axis=0, keepdims=True)
            stat_out[block] = jnp.broadcast_to(squares, (SUBS, LANES))
            if block == 0:
                stat_in[0] = stat_out[0]
            for dx in range(NX):
                if (block, dx) != (0, 0):
                    stat_copy(block, dx).start()

    late_halves = remote(acts.at[1], acts.at[1], act_s, act_r.at[2], up)
    late_halves.wait_recv()
    begin(0)
    fwd_all = remote(acts.at[3], acts.at[3], fwd_s, fwd_r, up)
    fwd_all.wait_recv()
    begin(1)
    middle(0)
    middle(1)
    finish(0)
    finish(1)
    fin_all = remote(back_rows, final_in.at[pl.ds(0, NY - 1)], fin_s, fin_r, up)
    fin_all.wait_recv()

    for tile in range(SUBS):
        cut = slice(tile * LANES, (tile + 1) * LANES)
        from_rows = slice((tile // 2) * 64, (tile // 2) * 64 + 64)
        mixed = [final_in[2 * (tile % 2) + odd, from_rows, :].astype(F32) for odd in range(2)]
        value = jnp.concatenate(mixed, axis=0).T
        summed[:, cut] = value
        hidden_ref[:, cut] = value.astype(BF16)
    fifteen = stat_in.at[pl.ds(1, 15)]
    stat_all = remote(fifteen, fifteen, stat_s, stat_r, up)
    stat_all.wait_recv()
    total = tree_sum([stat_in[n] for n in range(16)])
    scale = lax.rsqrt(total * (1.0 / (NX * CHANS)) + 1e-05)
    scale = jnp.broadcast_to(scale[0:1, :], (ROWS, LANES)).T
    for tile in range(SUBS):
        cut = slice(tile * LANES, (tile + 1) * LANES)
        normed_ref[:, cut] = (summed[:, cut] * scale * gain_ref[tile : tile + 1, :]).astype(BF16)

    sib_all.wait_send()
    shards_all(6, 3, 0).wait_send()
    remote(acts.at[pl.ds(0, 2)], acts.at[pl.ds(0, 2)], act_s, act_r.at[2], up).wait_send()
    fwd_all.wait_send()
    for pair in range(2):
        far_all(pair).wait_send()
        near_all(pair).wait_send()
    fin_all.wait_send()
    stat_all.wait_send()


def shard_rows(slot, h):
    return pl.ds(pl.multiple_of(h * (NZ * 32) + slot * 32, 32), 32)


def tree_sum(terms):
    while len(terms) > 1:
        rest = [terms[-1]] if len(terms) % 2 else []
        terms = [a + b for a, b in zip(terms[0::2], terms[1::2])] + rest
    return terms[0]


def local(
    q_stream, k_stream, v_stream, short_filter, rates, residues, skip, prior_state, out_weight, residual, norm_gain
):
    vmem = pl.BlockSpec(memory_space=pltpu.VMEM)
    hbm = pl.BlockSpec(memory_space=pltpu.HBM)
    dma = pltpu.SemaphoreType.DMA
    wide = (ROWS * SUBS, LANES)
    params = (MODES * SUBS, LANES)
    pair = (2 * SUBS, LANES)
    rows = (ROWS, CHANS)
    scratch = [
        pltpu.VMEM(rows, BF16),
        pltpu.VMEM(rows, BF16),
        pltpu.VMEM(rows, BF16),
        pltpu.VMEM(short_filter.shape, F32),
        pltpu.VMEM((MODES, CHANS), F32),
        pltpu.VMEM((MODES, CHANS), F32),
        pltpu.VMEM((SUBS, LANES), F32),
        pltpu.VMEM((MODES, CHANS), F32),
        pltpu.VMEM(rows, BF16),
        pltpu.VMEM((SUBS, LANES), F32),
        pltpu.VMEM((3,) + wide, F32),
        pltpu.VMEM((3, 2 * SUBS, LANES), F32),
        pltpu.VMEM(wide, F32),
        pltpu.VMEM(wide, F32),
        pltpu.VMEM(wide, F32),
        pltpu.VMEM((9 * SUBS, LANES), F32),
        pltpu.VMEM(params, F32),
        pltpu.VMEM(params, F32),
        pltpu.VMEM(params, F32),
        pltpu.VMEM(params, F32),
        pltpu.VMEM(params, F32),
        pltpu.VMEM(params, F32),
        pltpu.VMEM(params, F32),
        pltpu.VMEM((NJ,) + pair, F32),
        pltpu.VMEM((NZ,) + pair, F32),
        pltpu.VMEM(pair, F32),
        pltpu.VMEM((NJ,) + pair, F32),
        pltpu.VMEM(params, F32),
        pltpu.VMEM((CHANS, CHANS), BF16),
        pltpu.VMEM((NY, ROWS, CHANS), BF16),
        pltpu.VMEM((4, LANES, 2 * ROWS), BF16),
        pltpu.VMEM((4, LANES, 2 * ROWS), BF16),
        pltpu.VMEM((4, BAND, 2 * ROWS), BF16),
        pltpu.VMEM((4, BAND, 2 * ROWS), BF16),
        pltpu.VMEM((2, CHANS, 2 * ROWS), F32),
        pltpu.VMEM((NY - 1, BAND, ROWS), BF16),
        pltpu.VMEM((NY, BAND, ROWS), BF16),
        pltpu.VMEM((NY, BAND, ROWS), BF16),
        pltpu.VMEM((NY - 1, BAND, ROWS), BF16),
        pltpu.VMEM((ROWS, CHANS), F32),
        pltpu.VMEM((NY, SUBS, LANES), F32),
        pltpu.VMEM((16, SUBS, LANES), F32),
    ]
    sems = [dma((11,))]
    for sent, got in (
        (0, 0), (0, 0), (NZ, NZ), (0, 0), (4, 10), (2, 2), (0, 3), (0, 0), (2, 2), (2, 2), (0, 0), (0, 0), (0, 0)
    ):
        sems += [dma((n,)) if n else dma(()) for n in (sent, got)]
    return pl.pallas_call(
        kernel,
        out_shape=(jax.ShapeDtypeStruct((ROWS, CHANS), BF16), jax.ShapeDtypeStruct((ROWS, CHANS), BF16)),
        in_specs=[hbm] * 11,
        out_specs=(vmem, vmem),
        scratch_shapes=scratch + sems,
        compiler_params=pltpu.CompilerParams(
            collective_id=0, has_side_effects=True, vmem_limit_bytes=63 * 1024 * 1024
        ),
        name="mixer",
    )(
        q_stream, k_stream, v_stream, short_filter, rates, residues, skip.reshape(SUBS, LANES), prior_state,
        out_weight.T, residual, norm_gain.reshape(SUBS, LANES),
    )


def solution(mesh):
    placed = (
        P("seq", "ch"),
        P("seq", "ch"),
        P("seq", "ch"),
        P(None, None, "ch"),
        P(None, "ch"),
        P(None, "ch"),
        P("ch"),
        P(None, "ch"),
        P("ch", "seq"),
        P("seq", "ch"),
        P("ch"),
    )
    return jax.shard_map(
        local,
        mesh=mesh,
        in_specs=placed,
        out_specs=(P("seq", "ch"), P("seq", "ch")),
        check_vma=False,
    )
```

profile of v0, /device:TPU:224, one launch (start us, length us, event | category | flops | bytes accessed | tf_op | source)
XLA Modules:
  0.0 70.0 jit_solution(4819500380940564172)
XLA Ops:
  0.6 66.9 %mixer.1 = (bf16[128,1024]{1,0:T(8,128)(2,1)}, bf16[128,1024]{1,0:T(8,128)(2,1)}) custom-call(bf16[128,1024]{1,0:T(8,128)(2,1)} %q_hbm.1, bf16[128,1024]{1,0:T(8,128)(2,1)} %k_hbm.1, bf16[128,1024]{1,0:T(8,128)(2,1)} %v_hbm.1, f32[3,3,1024]{2,1,0:T(4,128)} %taps_hbm.1, f32[16,1024]{1,0:T(8,128)} %rates_hbm.1, f32[16,1024]{1,0:T(8,128)} %residues_hbm.1, ...), custom_call_target="tpu_custom_call" | custom-call | tf_op jit(solution)/shard_map/mixer/pallas_call | solution.py:609
  67.5 0.0 copy-start
  67.6 1.7 %copy.15 = bf16[128,1024]{1,0:T(8,128)(2,1)} copy(bf16[128,1024]{1,0:T(8,128)(2,1)} %get-tuple-element.4) | data formatting | bytes 524288
  69.3 0.0 copy-done
  69.3 0.7 %copy.16 = bf16[128,1024]{1,0:T(8,128)(2,1)} copy(bf16[128,1024]{1,0:T(8,128)(2,1)S(1)} %copy-done) | data formatting | bytes 524288
Async XLA Ops:
  67.5 1.7 %copy-start = (bf16[128,1024]{1,0:T(8,128)(2,1)S(1)}, bf16[128,1024]{1,0:T(8,128)(2,1)}, u32[]{:S(2)}) copy-start(bf16[128,1024]{1,0:T(8,128)(2,1)} %get-tuple-element.5) | copy-start | bytes 786436
where the time goes:
time: 70.1 us; the launch traced here: 70 us
  Pallas kernels  66.9 us (95%)
  local copies, waits for them, and re-layouts  2.42 us (3%)
    pallas_call x1, Pallas kernels, local(): pl.pallas_call(kernel, out_shape=(jax.ShapeDtypeStruct((ROWS, CHANS), BF1...  66.9 us
    unnamed x4, local copies, waits for them, and re-layouts  2.42 us

commit v1 on v0

--- a/solution.py
+++ b/solution.py
@@ -336,7 +336,6 @@
         sib_give(1)
 
     steps(64, ROWS, output_step, outputs)
-    pl.when(late)(ring_last)
 
     @pl.loop(1, z + 1)
     def _(d):
@@ -392,7 +391,8 @@
     def _():
         ring_next(2)
         sib_give(1)
-        ring_last()
+
+    ring_last()
 
     pl.when(has_next)(halo_copy.wait_send)
     to_owner_all.wait_send()

time: 70.1 us -> 72.2 us (1.030)
  the two profiles are of different devices: /device:TPU:224 before, /device:TPU:1 now
where the time goes in v1:
time: 72.2 us; the launch traced here: 72.1 us
  Pallas kernels  69 us (96%)
  local copies, waits for them, and re-layouts  2.42 us (3%)
    pallas_call x1, Pallas kernels, local(): pl.pallas_call(kernel, out_shape=(jax.ShapeDtypeStruct((ROWS, CHANS), BF1...  69 us
    unnamed x4, local copies, waits for them, and re-layouts  2.42 us

profile of v1, /device:TPU:1, one launch (start us, length us, event | category | flops | bytes accessed | tf_op | source)
XLA Modules:
  0.0 72.1 jit_solution(11914573590959526284)
XLA Ops:
  0.6 69.0 %mixer.1 = (bf16[128,1024]{1,0:T(8,128)(2,1)}, bf16[128,1024]{1,0:T(8,128)(2,1)}) custom-call(bf16[128,1024]{1,0:T(8,128)(2,1)} %q_hbm.1, bf16[128,1024]{1,0:T(8,128)(2,1)} %k_hbm.1, bf16[128,1024]{1,0:T(8,128)(2,1)} %v_hbm.1, f32[3,3,1024]{2,1,0:T(4,128)} %taps_hbm.1, f32[16,1024]{1,0:T(8,128)} %rates_hbm.1, f32[16,1024]{1,0:T(8,128)} %residues_hbm.1, ...), custom_call_target="tpu_custom_call" | custom-call | tf_op jit(solution)/shard_map/mixer/pallas_call | solution.py:609
  69.6 0.0 copy-start
  69.6 1.7 %copy.15 = bf16[128,1024]{1,0:T(8,128)(2,1)} copy(bf16[128,1024]{1,0:T(8,128)(2,1)} %get-tuple-element.4) | data formatting | bytes 524288
  71.4 0.0 copy-done
  71.4 0.7 copy.16
Async XLA Ops:
  69.6 1.7 %copy-start = (bf16[128,1024]{1,0:T(8,128)(2,1)S(1)}, bf16[128,1024]{1,0:T(8,128)(2,1)}, u32[]{:S(2)}) copy-start(bf16[128,1024]{1,0:T(8,128)(2,1)} %get-tuple-element.5) | copy-start | bytes 786436

commit v2 on v1

--- a/solution.py
+++ b/solution.py
@@ -336,6 +336,8 @@
         sib_give(1)
 
     steps(64, ROWS, output_step, outputs)
+    highest = z >= 12
+    pl.when(highest)(ring_last)
 
     @pl.loop(1, z + 1)
     def _(d):
@@ -392,7 +394,7 @@
         ring_next(2)
         sib_give(1)
 
-    ring_last()
+    pl.when(jnp.logical_not(highest))(ring_last)
 
     pl.when(has_next)(halo_copy.wait_send)
     to_owner_all.wait_send()

time: 72.2 us -> 68.1 us (0.943)
  Pallas kernels: 69 us -> 64.5 us
    pallas_call x1, Pallas kernels: 69 us -> 64.5 us  [local(): pl.pallas_call(kernel, out_shape=(jax.ShapeDtypeStruct((ROWS, CHANS), BF1...]
where the time goes in v2:
time: 68.1 us; the launch traced here: 67.6 us
  Pallas kernels  64.5 us (95%)
  local copies, waits for them, and re-layouts  2.42 us (4%)
    pallas_call x1, Pallas kernels, local(): pl.pallas_call(kernel, out_shape=(jax.ShapeDtypeStruct((ROWS, CHANS), BF1...  64.5 us
    unnamed x4, local copies, waits for them, and re-layouts  2.42 us

profile of v2, /device:TPU:1, one launch (start us, length us, event | category | flops | bytes accessed | tf_op | source)
XLA Modules:
  0.0 67.6 jit_solution(6684115939368634988)
XLA Ops:
  0.6 64.5 %mixer.1 = (bf16[128,1024]{1,0:T(8,128)(2,1)}, bf16[128,1024]{1,0:T(8,128)(2,1)}) custom-call(bf16[128,1024]{1,0:T(8,128)(2,1)} %q_hbm.1, bf16[128,1024]{1,0:T(8,128)(2,1)} %k_hbm.1, bf16[128,1024]{1,0:T(8,128)(2,1)} %v_hbm.1, f32[3,3,1024]{2,1,0:T(4,128)} %taps_hbm.1, f32[16,1024]{1,0:T(8,128)} %rates_hbm.1, f32[16,1024]{1,0:T(8,128)} %residues_hbm.1, ...), custom_call_target="tpu_custom_call" | custom-call | tf_op jit(solution)/shard_map/mixer/pallas_call | solution.py:611
  65.2 0.0 copy-start
  65.2 1.7 %copy.15 = bf16[128,1024]{1,0:T(8,128)(2,1)} copy(bf16[128,1024]{1,0:T(8,128)(2,1)} %get-tuple-element.4) | data formatting | bytes 524288
  66.9 0.0 copy-done
  66.9 0.7 %copy.16 = bf16[128,1024]{1,0:T(8,128)(2,1)} copy(bf16[128,1024]{1,0:T(8,128)(2,1)S(1)} %copy-done) | data formatting | bytes 524288
Async XLA Ops:
  65.2 1.7 %copy-start = (bf16[128,1024]{1,0:T(8,128)(2,1)S(1)}, bf16[128,1024]{1,0:T(8,128)(2,1)}, u32[]{:S(2)}) copy-start(bf16[128,1024]{1,0:T(8,128)(2,1)} %get-tuple-element.5) | copy-start | bytes 786436

commit v3 on v2

--- a/solution.py
+++ b/solution.py
@@ -417,7 +417,6 @@
     for part in range(2):
         act_copy(part, part).wait_recv()
         fwd_copy(part).start()
-    shards_wait(6, 9)
     twelve = weights.at[pl.ds(0, 12 * 32), :]
     sib_all = remote(twelve, twelve, sib_s.at[1], sib_r.at[1], sibling)
     sib_all.wait_recv()
@@ -425,9 +424,24 @@
     right, left = device(z, j, lax.rem(x + 1, NX)), device(z, j, lax.rem(x + 3, NX))
     sides = (right, left)
 
-    def project(pair):
+    def project(rows, weight):
+        return lax.dot_general(weight, rows, (((1,), (1,)), ((), ())), preferred_element_type=F32)
+
+    last_slots = [(core * NZ * 32 + 7 * 32, 3 * 32) for core in range(2)]
+    other_slots = ((0, 224), (320, 416), (832, 192))
+
+    def project_others(pair):
         rows = acts[2 * pair : 2 * pair + 2].reshape(2 * ROWS, CHANS)
-        parts[pair] = lax.dot_general(weights[...], rows, (((1,), (1,)), ((), ())), preferred_element_type=F32)
+        for at, count in other_slots:
+            parts[pair, at : at + count, :] = project(rows, weights[at : at + count, :])
+
+    def project_last():
+        rows = acts[...].reshape(NY * ROWS, CHANS)
+        some = jnp.concatenate([weights[at : at + count, :] for at, count in last_slots], axis=0)
+        value = project(rows, some)
+        for pair in range(2):
+            for n, (at, count) in enumerate(last_slots):
+                parts[pair, at : at + count, :] = value[n * count : (n + 1) * count, 2 * pair * ROWS : 2 * (pair + 1) * ROWS]
 
     def band(pair, dx):
         first = lax.rem(x + dx, NX) * 4 + NZ - z
@@ -451,7 +465,6 @@
         return remote(both, both, near_s.at[pair], near_r.at[pair], right)
 
     def begin(pair):
-        project(pair)
         chunks = band(pair, 2)
         for side in range(2):
             for i in range(4):
@@ -499,9 +512,13 @@
 
     late_halves = remote(acts.at[1], acts.at[1], act_s, act_r.at[2], up)
     late_halves.wait_recv()
-    begin(0)
+    project_others(0)
     fwd_all = remote(acts.at[3], acts.at[3], fwd_s, fwd_r, up)
     fwd_all.wait_recv()
+    project_others(1)
+    shards_wait(6, 9)
+    project_last()
+    begin(0)
     begin(1)
     middle(0)
     middle(1)
@@ -517,6 +534,15 @@
         value = jnp.concatenate(mixed, axis=0).T
         summed[:, cut] = value
         hidden_ref[:, cut] = value.astype(BF16)
+    sib_all.wait_send()
+    shards_all(6, 3, 0).wait_send()
+    remote(acts.at[pl.ds(0, 2)], acts.at[pl.ds(0, 2)], act_s, act_r.at[2], up).wait_send()
+    fwd_all.wait_send()
+    for pair in range(2):
+        far_all(pair).wait_send()
+        near_all(pair).wait_send()
+    fin_all.wait_send()
+
     fifteen = stat_in.at[pl.ds(1, 15)]
     stat_all = remote(fifteen, fifteen, stat_s, stat_r, up)
     stat_all.wait_recv()
@@ -526,15 +552,6 @@
     for tile in range(SUBS):
         cut = slice(tile * LANES, (tile + 1) * LANES)
         normed_ref[:, cut] = (summed[:, cut] * scale * gain_ref[tile : tile + 1, :]).astype(BF16)
-
-    sib_all.wait_send()
-    shards_all(6, 3, 0).wait_send()
-    remote(acts.at[pl.ds(0, 2)], acts.at[pl.ds(0, 2)], act_s, act_r.at[2], up).wait_send()
-    fwd_all.wait_send()
-    for pair in range(2):
-        far_all(pair).wait_send()
-        near_all(pair).wait_send()
-    fin_all.wait_send()
     stat_all.wait_send()
 
 

time: 68.1 us -> 68 us (level); the launches traced: 67.6 us -> 66.8 us
  Pallas kernels: 64.5 us -> 63.7 us
    pallas_call x1, Pallas kernels: 64.5 us -> 63.7 us  [local(): pl.pallas_call(kernel, out_shape=(jax.ShapeDtypeStruct((ROWS, CHANS), BF1...]
where the time goes in v3:
time: 68 us; the launch traced here: 66.8 us
  Pallas kernels  63.7 us (94%)
  local copies, waits for them, and re-layouts  2.42 us (4%)
    pallas_call x1, Pallas kernels, local(): pl.pallas_call(kernel, out_shape=(jax.ShapeDtypeStruct((ROWS, CHANS), BF1...  63.7 us
    unnamed x4, local copies, waits for them, and re-layouts  2.42 us

profile of v3, /device:TPU:1, one launch (start us, length us, event | category | flops | bytes accessed | tf_op | source)
XLA Modules:
  0.0 66.8 jit_solution(554643265064341624)
XLA Ops:
  0.6 63.7 %mixer.1 = (bf16[128,1024]{1,0:T(8,128)(2,1)}, bf16[128,1024]{1,0:T(8,128)(2,1)}) custom-call(bf16[128,1024]{1,0:T(8,128)(2,1)} %q_hbm.1, bf16[128,1024]{1,0:T(8,128)(2,1)} %k_hbm.1, bf16[128,1024]{1,0:T(8,128)(2,1)} %v_hbm.1, f32[3,3,1024]{2,1,0:T(4,128)} %taps_hbm.1, f32[16,1024]{1,0:T(8,128)} %rates_hbm.1, f32[16,1024]{1,0:T(8,128)} %residues_hbm.1, ...), custom_call_target="tpu_custom_call" | custom-call | tf_op jit(solution)/shard_map/mixer/pallas_call | solution.py:628
  64.4 0.0 copy-start
  64.4 1.7 %copy.15 = bf16[128,1024]{1,0:T(8,128)(2,1)} copy(bf16[128,1024]{1,0:T(8,128)(2,1)} %get-tuple-element.4) | data formatting | bytes 524288
  66.1 0.0 copy-done
  66.1 0.7 %copy.16 = bf16[128,1024]{1,0:T(8,128)(2,1)} copy(bf16[128,1024]{1,0:T(8,128)(2,1)S(1)} %copy-done) | data formatting | bytes 524288
Async XLA Ops:
  64.4 1.7 %copy-start = (bf16[128,1024]{1,0:T(8,128)(2,1)S(1)}, bf16[128,1024]{1,0:T(8,128)(2,1)}, u32[]{:S(2)}) copy-start(bf16[128,1024]{1,0:T(8,128)(2,1)} %get-tuple-element.5) | copy-start | bytes 786436

commit v4 on v3

--- a/solution.py
+++ b/solution.py
@@ -129,14 +129,17 @@
         for d in (2, 1):
             ring_copy(shard(far), -d, far + d, step, got + 1 if d == 2 else got + 2).start()
 
-    def ring_last():
-        shards_wait(1, 6)
-        shards_wait(1, 7)
+    def ring_last(side):
+        shards_wait(1, 6 + side)
+        src, hops, slot = ((shard(NZ - 6), 1, NZ - 7), (shard(6), -1, 7))[side]
+
+        @pl.when(h == side)
+        def _():
+            for core in (h, 1 - h):
+                ring_copy(src, 2 * hops, 8, 3, 9, core).start()
+
         for core in (h, 1 - h):
-            ring_copy(shard(NZ - 6 - 4 * h), 2 - 4 * h, 8, 3, 9, core).start()
-        for core in (h, 1 - h):
-            ring_copy(shard(NZ - 6), 1, NZ - 7, 3, 9, core).start()
-            ring_copy(shard(6), -1, 7, 3, 9, core).start()
+            ring_copy(src, hops, slot, 3, 9, core).start()
 
     def sib_copy(slot):
         two = weights.at[pl.ds(pl.multiple_of(h * (NZ * 32) + slot * 32, 32), 2 * 32), :]
@@ -336,8 +339,11 @@
         sib_give(1)
 
     steps(64, ROWS, output_step, outputs)
-    highest = z >= 12
-    pl.when(highest)(ring_last)
+    highest = z >= 14
+
+    @pl.when(highest)
+    def _():
+        ring_last(0)
 
     @pl.loop(1, z + 1)
     def _(d):
@@ -394,7 +400,11 @@
         ring_next(2)
         sib_give(1)
 
-    pl.when(jnp.logical_not(highest))(ring_last)
+    @pl.when(jnp.logical_not(highest))
+    def _():
+        ring_last(0)
+
+    ring_last(1)
 
     pl.when(has_next)(halo_copy.wait_send)
     to_owner_all.wait_send()

time: 68 us -> 67.3 us (0.990)
  the two profiles are of different devices: /device:TPU:1 before, /device:TPU:32 now
where the time goes in v4:
time: 67.3 us; the launch traced here: 67.1 us
  Pallas kernels  64.1 us (95%)
  local copies, waits for them, and re-layouts  2.42 us (4%)
    pallas_call x1, Pallas kernels, local(): pl.pallas_call(kernel, out_shape=(jax.ShapeDtypeStruct((ROWS, CHANS), BF1...  64.1 us
    unnamed x4, local copies, waits for them, and re-layouts  2.42 us

profile of v4, /device:TPU:32, one launch (start us, length us, event | category | flops | bytes accessed | tf_op | source)
XLA Modules:
  0.0 67.1 jit_solution(701115715903459855)
XLA Ops:
  0.6 64.1 %mixer.1 = (bf16[128,1024]{1,0:T(8,128)(2,1)}, bf16[128,1024]{1,0:T(8,128)(2,1)}) custom-call(bf16[128,1024]{1,0:T(8,128)(2,1)} %q_hbm.1, bf16[128,1024]{1,0:T(8,128)(2,1)} %k_hbm.1, bf16[128,1024]{1,0:T(8,128)(2,1)} %v_hbm.1, f32[3,3,1024]{2,1,0:T(4,128)} %taps_hbm.1, f32[16,1024]{1,0:T(8,128)} %rates_hbm.1, f32[16,1024]{1,0:T(8,128)} %residues_hbm.1, ...), custom_call_target="tpu_custom_call" | custom-call | tf_op jit(solution)/shard_map/mixer/pallas_call | solution.py:638
  64.7 0.0 copy-start
  64.7 1.7 %copy.15 = bf16[128,1024]{1,0:T(8,128)(2,1)} copy(bf16[128,1024]{1,0:T(8,128)(2,1)} %get-tuple-element.4) | data formatting | bytes 524288
  66.4 0.0 copy-done
  66.4 0.7 %copy.16 = bf16[128,1024]{1,0:T(8,128)(2,1)} copy(bf16[128,1024]{1,0:T(8,128)(2,1)S(1)} %copy-done) | data formatting | bytes 524288
Async XLA Ops:
  64.7 1.7 %copy-start = (bf16[128,1024]{1,0:T(8,128)(2,1)S(1)}, bf16[128,1024]{1,0:T(8,128)(2,1)}, u32[]{:S(2)}) copy-start(bf16[128,1024]{1,0:T(8,128)(2,1)} %get-tuple-element.5) | copy-start | bytes 786436

commit v5 on v4

--- a/solution.py
+++ b/solution.py
@@ -400,10 +400,17 @@
         ring_next(2)
         sib_give(1)
 
+    def forward(part):
+        act_copy(part, part).wait_recv()
+        fwd_copy(part).start()
+
+    forward(0)
+
     @pl.when(jnp.logical_not(highest))
     def _():
         ring_last(0)
 
+    forward(1)
     ring_last(1)
 
     pl.when(has_next)(halo_copy.wait_send)
@@ -424,9 +431,6 @@
     res_all = remote(res_in, res_in, res_s, res_r, sibling)
     res_all.wait_send()
     res_all.wait_recv()
-    for part in range(2):
-        act_copy(part, part).wait_recv()
-        fwd_copy(part).start()
     twelve = weights.at[pl.ds(0, 12 * 32), :]
     sib_all = remote(twelve, twelve, sib_s.at[1], sib_r.at[1], sibling)
     sib_all.wait_recv()
@@ -445,13 +449,12 @@
         for at, count in other_slots:
             parts[pair, at : at + count, :] = project(rows, weights[at : at + count, :])
 
-    def project_last():
-        rows = acts[...].reshape(NY * ROWS, CHANS)
+    def project_last(pair):
+        rows = acts[2 * pair : 2 * pair + 2].reshape(2 * ROWS, CHANS)
         some = jnp.concatenate([weights[at : at + count, :] for at, count in last_slots], axis=0)
         value = project(rows, some)
-        for pair in range(2):
-            for n, (at, count) in enumerate(last_slots):
-                parts[pair, at : at + count, :] = value[n * count : (n + 1) * count, 2 * pair * ROWS : 2 * (pair + 1) * ROWS]
+        for n, (at, count) in enumerate(last_slots):
+            parts[pair, at : at + count, :] = value[n * count : (n + 1) * count, :]
 
     def band(pair, dx):
         first = lax.rem(x + dx, NX) * 4 + NZ - z
@@ -523,12 +526,13 @@
     late_halves = remote(acts.at[1], acts.at[1], act_s, act_r.at[2], up)
     late_halves.wait_recv()
     project_others(0)
+    shards_wait(6, 9)
+    project_last(0)
+    begin(0)
     fwd_all = remote(acts.at[3], acts.at[3], fwd_s, fwd_r, up)
     fwd_all.wait_recv()
     project_others(1)
-    shards_wait(6, 9)
-    project_last()
-    begin(0)
+    project_last(1)
     begin(1)
     middle(0)
     middle(1)

time: 67.3 us -> 67.6 us (level)
  the two profiles are of different devices: /device:TPU:32 before, /device:TPU:96 now
where the time goes in v5:
time: 67.6 us; the launch traced here: 67.4 us
  Pallas kernels  64.4 us (95%)
  local copies, waits for them, and re-layouts  2.42 us (4%)
    pallas_call x1, Pallas kernels, local(): pl.pallas_call(kernel, out_shape=(jax.ShapeDtypeStruct((ROWS, CHANS), BF1...  64.4 us
    unnamed x4, local copies, waits for them, and re-layouts  2.42 us

profile of v5, /device:TPU:96, one launch (start us, length us, event | category | flops | bytes accessed | tf_op | source)
XLA Modules:
  0.0 67.4 jit_solution(5071574051184634389)
XLA Ops:
  0.6 64.4 %mixer.1 = (bf16[128,1024]{1,0:T(8,128)(2,1)}, bf16[128,1024]{1,0:T(8,128)(2,1)}) custom-call(bf16[128,1024]{1,0:T(8,128)(2,1)} %q_hbm.1, bf16[128,1024]{1,0:T(8,128)(2,1)} %k_hbm.1, bf16[128,1024]{1,0:T(8,128)(2,1)} %v_hbm.1, f32[3,3,1024]{2,1,0:T(4,128)} %taps_hbm.1, f32[16,1024]{1,0:T(8,128)} %rates_hbm.1, f32[16,1024]{1,0:T(8,128)} %residues_hbm.1, ...), custom_call_target="tpu_custom_call" | custom-call | tf_op jit(solution)/shard_map/mixer/pallas_call | solution.py:642
  65.0 0.0 copy-start
  65.0 1.7 %copy.15 = bf16[128,1024]{1,0:T(8,128)(2,1)} copy(bf16[128,1024]{1,0:T(8,128)(2,1)} %get-tuple-element.4) | data formatting | bytes 524288
  66.7 0.0 copy-done
  66.7 0.7 %copy.16 = bf16[128,1024]{1,0:T(8,128)(2,1)} copy(bf16[128,1024]{1,0:T(8,128)(2,1)S(1)} %copy-done) | data formatting | bytes 524288
Async XLA Ops:
  65.0 1.7 %copy-start = (bf16[128,1024]{1,0:T(8,128)(2,1)S(1)}, bf16[128,1024]{1,0:T(8,128)(2,1)}, u32[]{:S(2)}) copy-start(bf16[128,1024]{1,0:T(8,128)(2,1)} %get-tuple-element.5) | copy-start | bytes 786436

commit v6 on v5

--- a/solution.py
+++ b/solution.py
@@ -404,13 +404,10 @@
         act_copy(part, part).wait_recv()
         fwd_copy(part).start()
 
-    forward(0)
-
     @pl.when(jnp.logical_not(highest))
     def _():
         ring_last(0)
 
-    forward(1)
     ring_last(1)
 
     pl.when(has_next)(halo_copy.wait_send)
@@ -421,6 +418,8 @@
     def _(d):
         along_line(d).wait_send()
 
+    forward(0)
+    forward(1)
     sib_give(2)
     sib_give(3)
     own_all = remote(weight_hbm, own_weights, sib_s.at[0], sib_r.at[0], sibling)

time: 67.6 us -> 67.3 us (level)
  the two profiles are of different devices: /device:TPU:96 before, /device:TPU:32 now
where the time goes in v6:
time: 67.3 us; the launch traced here: 67.2 us
  Pallas kernels  64.1 us (95%)
  local copies, waits for them, and re-layouts  2.42 us (4%)
    pallas_call x1, Pallas kernels, local(): pl.pallas_call(kernel, out_shape=(jax.ShapeDtypeStruct((ROWS, CHANS), BF1...  64.1 us
    unnamed x4, local copies, waits for them, and re-layouts  2.42 us

profile of v6, /device:TPU:32, one launch (start us, length us, event | category | flops | bytes accessed | tf_op | source)
XLA Modules:
  0.0 67.2 jit_solution(6917205875590388036)
XLA Ops:
  0.6 64.1 %mixer.1 = (bf16[128,1024]{1,0:T(8,128)(2,1)}, bf16[128,1024]{1,0:T(8,128)(2,1)}) custom-call(bf16[128,1024]{1,0:T(8,128)(2,1)} %q_hbm.1, bf16[128,1024]{1,0:T(8,128)(2,1)} %k_hbm.1, bf16[128,1024]{1,0:T(8,128)(2,1)} %v_hbm.1, f32[3,3,1024]{2,1,0:T(4,128)} %taps_hbm.1, f32[16,1024]{1,0:T(8,128)} %rates_hbm.1, f32[16,1024]{1,0:T(8,128)} %residues_hbm.1, ...), custom_call_target="tpu_custom_call" | custom-call | tf_op jit(solution)/shard_map/mixer/pallas_call | solution.py:641
  64.7 0.0 copy-start
  64.7 1.7 %copy.15 = bf16[128,1024]{1,0:T(8,128)(2,1)} copy(bf16[128,1024]{1,0:T(8,128)(2,1)} %get-tuple-element.4) | data formatting | bytes 524288
  66.4 0.0 copy-done
  66.4 0.7 %copy.16 = bf16[128,1024]{1,0:T(8,128)(2,1)} copy(bf16[128,1024]{1,0:T(8,128)(2,1)S(1)} %copy-done) | data formatting | bytes 524288
Async XLA Ops:
  64.7 1.7 %copy-start = (bf16[128,1024]{1,0:T(8,128)(2,1)S(1)}, bf16[128,1024]{1,0:T(8,128)(2,1)}, u32[]{:S(2)}) copy-start(bf16[128,1024]{1,0:T(8,128)(2,1)} %get-tuple-element.5) | copy-start | bytes 786436
